TPU v7x, 32 devices: a whole 2x2x4 slice. The times are simulated.
32 devices in a mesh: row: 4 (over y, x), col: 2 (over core), layer: 4 (over z).
Axes of the slice: x: 2, y: 2, z: 4, core: 2. Of those that a mesh axis runs over, the one named last changes fastest.
Arguments:
- a_blocks: bfloat16 [4, 2, 16, 64, 512], P('layer', None, ('row', 'col')), may hold values from -0.09375 to 0.09375
- a_cols: int32 [4, 2, 16, 8], P('layer', None, ('row', 'col')), may hold values from 0 to 7
- p_blocks: bfloat16 [4, 2, 2, 8, 64, 256], P('layer', None, 'col', 'row'), may hold values from -12 to 12
- p_cols: int32 [4, 2, 2, 8, 4], P('layer', None, 'col', 'row'), may hold values from 0 to 15, as said below
- c_cols: int32 [2, 16, 8], P('col', 'row'), may hold values from 0 to 15, as said below
Outputs:
- c_blocks: bfloat16 [2, 16, 64, 512], P('col', ('row', 'layer'))
Inputs may be any that keep to these rules, and one draw needn't show every extreme that they name: `p_cols`: the 4 entries of a block row of P in one column group are distinct. `c_cols`: the 8 entries of a block row of C in one column group are distinct.
All inputs are finite; a program needn't handle non-finite values.
Results may differ from a plain program's by a relative error of at most 0.008.
Values may be sent and summed in bfloat16 or wider, within the bound.
A program may use at most 64 MiB of HBM per device.

v0:
```python
import functools

import jax
import jax.numpy as jnp
from jax import lax
from jax.experimental import pallas as pl
from jax.experimental.pallas import tpu as pltpu
from jax.sharding import PartitionSpec as P

MESH = pl.DeviceIdType.MESH
LANES = 128
NCC = 16


def partner(me, d, n):
    out = 0
    bit = 1
    while bit < n:
        out = out + lax.rem(lax.div(me, bit) + ((d // bit) % 2), 2) * bit
        bit *= 2
    return out


def pair_codes(values, half):
    lane = lax.broadcasted_iota(jnp.int32, (1, LANES), 1)
    low = lane < half
    codes = []
    for p in range(len(values) // 2):
        codes.append(jnp.where(low, values[2 * p], values[2 * p + 1]))
        codes.append(jnp.where(low, values[2 * p + 1], values[2 * p]))
    return codes


def pair_tiles(x, half):
    tiles = []
    for p in range(x.shape[1] // LANES):
        tile = x[:, p * LANES:(p + 1) * LANES].astype(jnp.float32)
        tiles.append(tile)
        tiles.append(pltpu.roll(tile, half, axis=1))
    return tiles


def select4(lane, q, parts):
    out = parts[3]
    for g in (2, 1, 0):
        out = jnp.where(lane < (g + 1) * q, parts[g], out)
    return out


ORDER = (0, 2, 1, 3)


def pack(t0, t1, even, q):
    return jnp.where(even, t0, pltpu.roll(t1, q, axis=1)), jnp.where(even, pltpu.roll(t0, LANES - q, axis=1), t1)


def kernel(dims, a_hbm, a_cols_hbm, p_hbm, p_cols_hbm, c_cols_hbm, out_ref,
           a_cols, p_cols, c_cols, a_v, p_v, p_all, code_all, at_all, spread, t_acc, t_pick, own, c_send, c_recv,
           in_sem, ps, pr, cs, cr, as_, ar, zs, zr):
    n_row, n_col, n_layer = dims
    sections, rl, side, width = a_v.shape
    rp = p_all.shape[3]
    group = at_all.shape[0] * rl
    own_rows = c_send.shape[2]
    kc = c_cols.shape[2]
    quarter = side // 2
    tiles_t = NCC * quarter // LANES
    my_row, my_col, my_layer = (lax.axis_index(x) for x in ("row", "col", "layer"))

    barrier = pltpu.get_barrier_semaphore()
    for axis, me, n in (("row", my_row, n_row), ("col", my_col, n_col), ("layer", my_layer, n_layer)):
        for d in range(1, n):
            pl.semaphore_signal(barrier, inc=1, device_id={axis: partner(me, d, n)}, device_id_type=MESH)

    load_p = pltpu.make_async_copy(p_hbm.at[0, :, 0], p_v, in_sem.at[0])
    load_a = pltpu.make_async_copy(a_hbm.at[0], a_v, in_sem.at[1])
    load_pc = pltpu.make_async_copy(p_cols_hbm, p_cols, in_sem.at[2])
    load_ac = pltpu.make_async_copy(a_cols_hbm, a_cols, in_sem.at[3])
    load_cc = pltpu.make_async_copy(c_cols_hbm, c_cols, in_sem.at[4])
    for load in (load_p, load_pc, load_a, load_ac, load_cc):
        load.start()

    lane = lax.broadcasted_iota(jnp.int32, (side, LANES), 1)
    lane1 = lax.broadcasted_iota(jnp.int32, (1, LANES), 1)
    even = lax.rem(lax.div(lane, quarter), 2) == 0
    second = jnp.where(lane < side, 0, 1)
    fourth = lax.div(lane, quarter)

    load_pc.wait()
    for s in range(sections):
        for r in range(rp):
            cols = [p_cols[0, s, 0, r, j] for j in range(4)]
            for k in range(4):
                code = select4(lane1, quarter, [cols[ORDER[(g - k) % 4]] for g in range(4)])
                at = (s * rp + r) * 4 + k
                code_all[my_row, at:at + 1, :] = code
    load_p.wait()
    for s in range(sections):
        for r in range(rp):
            x = p_v[s, r].astype(jnp.float32)
            halves = pack(x[:, :LANES], x[:, LANES:], even, quarter)
            for h in range(2):
                p_all[h, my_row, s, r] = halves[h].astype(jnp.bfloat16)

    load_cc.wait()
    pl.semaphore_wait(barrier, (n_row - 1) + (n_col - 1) + (n_layer - 1))

    sends = []
    p_copies = [[], []]
    code_copies = []
    for d in range(1, n_row):
        to = {"row": partner(my_row, d, n_row)}
        code_copies.append(pltpu.make_async_remote_copy(
            code_all.at[my_row], code_all.at[my_row], cs.at[d - 1], cr.at[d - 1], device_id=to, device_id_type=MESH))
        for h in range(2):
            p_copies[h].append(pltpu.make_async_remote_copy(
                p_all.at[h, my_row], p_all.at[h, my_row], ps.at[h, d - 1], pr.at[h, d - 1],
                device_id=to, device_id_type=MESH))
    for copy in code_copies + p_copies[0] + p_copies[1]:
        copy.start()
        sends.append(copy)

    load_ac.wait()
    load_a.wait()
    for s in range(sections):
        for i in range(rl):
            codes = pair_codes([a_cols[0, s, i, k] for k in range(width // side)], side)
            codes = [jnp.broadcast_to(code, (side, LANES)) for code in codes]
            tiles = pair_tiles(a_v[s, i], side)
            for q in range(n_row * rp // 2):
                total = jnp.zeros((side, LANES), jnp.float32)
                for code, tile in zip(codes, tiles):
                    total = total + jnp.where(code == 2 * q + second, tile, 0.0)
                slot = 2 * q // rp
                start = (s * rp + 2 * q % rp) * side
                at_all[my_col, slot, i * side:(i + 1) * side, start:start + LANES] = total.astype(jnp.bfloat16)
    a_copies = []
    for d in range(1, n_col):
        copy = pltpu.make_async_remote_copy(
            at_all.at[my_col], at_all.at[my_col], as_.at[d - 1], ar.at[d - 1],
            device_id={"col": partner(my_col, d, n_col)}, device_id_type=MESH)
        copy.start()
        a_copies.append(copy)
        sends.append(copy)

    def spread_rows(h, slot, to):
        for s in range(sections):
            for r in range(rp):
                tile = p_all[h, slot, s, r].astype(jnp.float32)
                tiles = [tile] + [pltpu.roll(tile, k * quarter, axis=1) for k in range(1, 4)]
                codes = []
                for k in range(4):
                    at = (s * rp + r) * 4 + k
                    codes.append(jnp.broadcast_to(code_all[slot, at:at + 1, :], (side, LANES)))
                for q in range(tiles_t):
                    total = jnp.zeros((side, LANES), jnp.float32)
                    for code, turned in zip(codes, tiles):
                        total = jnp.where(code == 4 * q + fourth, turned, total)
                    first = (s * rp + r) * side
                    spread[h, to, first:first + side, q * LANES:(q + 1) * LANES] = total.astype(jnp.bfloat16)

    step_cols = 2 * LANES

    def multiply(h, d):
        left = at_all[:, partner(my_row, d, n_row)].reshape(group * side, sections * rp * side)
        for n in range(0, NCC * quarter, step_cols):
            part = jnp.dot(left, spread[h, d, :, n:n + step_cols], preferred_element_type=jnp.float32)
            part = part.reshape(group, side, step_cols)
            if d > 0:
                part = part + t_acc[h, :, :, n:n + step_cols]
            t_acc[h, :, :, n:n + step_cols] = part

    def turn_row(h, i):
        for q in range(tiles_t):
            tile = t_acc[h, i, :, q * LANES:(q + 1) * LANES]
            t_pick[h, i, q] = tile
            for k in range(1, 4):
                t_pick[h, i, k * tiles_t + q] = pltpu.roll(tile, k * quarter, axis=1)

    def pick(h, i, u):
        parts = []
        for g in range(4):
            c = c_cols[0, i, 4 * u + ORDER[g]]
            turn = lax.rem(g + 4 - lax.rem(c, 4), 4)
            parts.append(t_pick[h, i, turn * tiles_t + lax.div(c, 4)])
        return select4(lane, quarter, parts)

    def receive(h, d):
        if h == 0:
            code_copies[d - 1].wait_recv()
        p_copies[h][d - 1].wait_recv()
        spread_rows(h, partner(my_row, d, n_row), d)
        multiply(h, d)

    for h in range(2):
        spread_rows(h, my_row, 0)
    for copy in a_copies:
        copy.wait_recv()
    for h in range(2):
        multiply(h, 0)

    z_copies = [[], []]
    for h in range(2):
        for d in range(1, n_row):
            receive(h, d)
        for d in range(n_layer - 1, 0, -1):
            dst = partner(my_layer, d, n_layer)
            for o in range(own_rows):
                turn_row(h, dst * own_rows + o)
                for u in range(kc // 4):
                    c_send[h, d - 1, o, :, u * LANES:(u + 1) * LANES] = pick(
                        h, dst * own_rows + o, u).astype(jnp.bfloat16)
            copy = pltpu.make_async_remote_copy(
                c_send.at[h, d - 1], c_recv.at[h, d - 1], zs.at[h, d - 1], zr.at[h, d - 1],
                device_id={"layer": dst}, device_id_type=MESH)
            copy.start()
            z_copies[h].append(copy)
            sends.append(copy)
        for o in range(own_rows):
            turn_row(h, my_layer * own_rows + o)
            for u in range(kc // 4):
                own[h, o, :, u * LANES:(u + 1) * LANES] = pick(h, my_layer * own_rows + o, u)

    for h in range(2):
        for copy in z_copies[h]:
            copy.wait_recv()
        total = own[h]
        for d in range(1, n_layer):
            total = total + c_recv[h, d - 1].astype(jnp.float32)
        own[h] = total
    for o in range(own_rows):
        for u in range(kc // 4):
            h0 = own[0, o, :, u * LANES:(u + 1) * LANES]
            h1 = own[1, o, :, u * LANES:(u + 1) * LANES]
            for e, tile in enumerate(pack(h0, h1, even, quarter)):
                at = (2 * u + e) * LANES
                out_ref[0, o, :, at:at + LANES] = tile.astype(jnp.bfloat16)
    for copy in sends:
        copy.wait_send()


def local(dims, a_blocks, a_cols, p_blocks, p_cols, c_cols):
    n_row, n_col, n_layer = dims
    sections, rl, side, width = a_blocks.shape[1:]
    rp, p_width = p_blocks.shape[3], p_blocks.shape[5]
    group, kc = c_cols.shape[1:]
    own_rows = group // n_layer
    strip = (own_rows, side, kc * side)
    half_strip = (own_rows, side, kc * side // 2)
    depth = sections * rp * side
    dma = pltpu.SemaphoreType.DMA
    return pl.pallas_call(
        functools.partial(kernel, dims),
        out_shape=jax.ShapeDtypeStruct((1,) + strip, jnp.bfloat16),
        in_specs=[pl.BlockSpec(memory_space=pl.ANY)] * 5,
        out_specs=pl.BlockSpec(memory_space=pltpu.VMEM),
        scratch_shapes=[
            pltpu.SMEM(a_cols.shape, jnp.int32),
            pltpu.SMEM(p_cols.shape, jnp.int32),
            pltpu.SMEM(c_cols.shape, jnp.int32),
            pltpu.VMEM((sections, rl, side, width), jnp.bfloat16),
            pltpu.VMEM((sections, rp, side, p_width), jnp.bfloat16),
            pltpu.VMEM((2, n_row, sections, rp, side, LANES), jnp.bfloat16),
            pltpu.VMEM((n_row, sections * rp * 4, LANES), jnp.int32),
            pltpu.VMEM((n_col, n_row, rl * side, depth), jnp.bfloat16),
            pltpu.VMEM((2, n_row, depth, NCC * side // 2), jnp.bfloat16),
            pltpu.VMEM((2, group, side, NCC * side // 2), jnp.float32),
            pltpu.VMEM((2, group, NCC, side, LANES), jnp.float32),
            pltpu.VMEM((2,) + half_strip, jnp.float32),
            pltpu.VMEM((2, n_layer - 1) + half_strip, jnp.bfloat16),
            pltpu.VMEM((2, n_layer - 1) + half_strip, jnp.bfloat16),
            dma((5,)),
            dma((2, n_row - 1)), dma((2, n_row - 1)),
            dma((n_row - 1,)), dma((n_row - 1,)),
            dma((n_col - 1,)), dma((n_col - 1,)),
            dma((2, n_layer - 1)), dma((2, n_layer - 1)),
        ],
        compiler_params=pltpu.CompilerParams(
            collective_id=0, has_side_effects=True, vmem_limit_bytes=63 * 2**20),
    )(a_blocks, a_cols, p_blocks, p_cols, c_cols)


def solution(mesh):
    dims = tuple(mesh.shape[x] for x in ("row", "col", "layer"))
    return jax.shard_map(
        functools.partial(local, dims),
        mesh=mesh,
        in_specs=(
            P("layer", None, ("row", "col"), None, None),
            P("layer", None, ("row", "col"), None),
            P("layer", None, "col", "row", None, None),
            P("layer", None, "col", "row", None),
            P("col", "row", None),
        ),
        out_specs=P("col", ("row", "layer"), None, None),
        check_vma=False,
    )
```

profile of v0, /device:TPU:0, one launch (start us, length us, event | category | flops | bytes accessed | tf_op | source)
XLA Modules:
  0.0 21.3 jit_solution(16447634764153510743)
XLA Ops:
  0.0 19.8 %shard_map.55 = bf16[1,1,64,512]{3,2,1,0:T(8,128)(2,1)} custom-call(bf16[1,2,2,64,512]{4,3,2,1,0:T(8,128)(2,1)} %a_hbm.1, s32[1,2,2,8]{3,2,1,0:T(2,128)} %a_cols_hbm.1, bf16[1,2,1,2,64,256]{5,4,3,2,1,0:T(8,128)(2,1)} %p_hbm.1, s32[1,2,1,2,4]{4,3,2,1,0:T(2,128)} %p_cols_hbm.1, s32[1,4,8]{2,1,0:T(4,128)} %c_cols_hbm.1), custom_call_target="tpu_custom_call" | custom-call | tf_op jit(solution)/shard_map/pallas_call | solution.py:252
  19.8 1.5 %copy.7 = bf16[1,1,64,512]{3,2,1,0:T(8,128)(2,1)} copy(bf16[1,1,64,512]{3,2,1,0:T(8,128)(2,1)} %shard_map.55) | data formatting | bytes 131072
where the time goes:
time: 21.5 us; the launch traced here: 21.3 us
  Pallas kernels  19.8 us (92%)
  local copies, waits for them, and re-layouts  1.47 us (7%)
    pallas_call x1, Pallas kernels, local(): pl.pallas_call(functools.partial(kernel, dims), out_shape=jax.ShapeDtypeS...  19.8 us
    unnamed x1, local copies, waits for them, and re-layouts  1.47 us

commit v1 on v0

--- a/solution.py
+++ b/solution.py
@@ -55,8 +55,8 @@
 
 
 def kernel(dims, a_hbm, a_cols_hbm, p_hbm, p_cols_hbm, c_cols_hbm, out_ref,
-           a_cols, p_cols, c_cols, a_v, p_v, p_all, code_all, at_all, spread, t_acc, t_pick, own, c_send, c_recv,
-           in_sem, ps, pr, cs, cr, as_, ar, zs, zr):
+           a_cols, p_cols, c_cols, a_v, p_v, p_all, code_all, at_all, spread, t_acc, t_pick, own, c_send, c_recv, via,
+           in_sem, ps, pr, cs, cr, as_, ar, zs, zr, vs, vr):
     n_row, n_col, n_layer = dims
     sections, rl, side, width = a_v.shape
     rp = p_all.shape[3]
@@ -199,10 +199,44 @@
     for h in range(2):
         multiply(h, 0)
 
-    z_copies = [[], []]
+    chained = n_layer == 4
+    at_end = lax.rem(lax.div(my_layer + 1, 2), 2) == 0
+    inside = jnp.logical_not(at_end)
+
+    direct = [{}, {}]
+    handed = []
+    for h in range(2):
+        for d in range(1, n_layer):
+            direct[h][d] = pltpu.make_async_remote_copy(
+                c_send.at[h, d - 1], c_recv.at[h, d - 1], zs.at[h, d - 1], zr.at[h, d - 1],
+                device_id={"layer": partner(my_layer, d, n_layer)}, device_id_type=MESH)
+        if chained:
+            handed.append(pltpu.make_async_remote_copy(
+                c_send.at[h, 2], via.at[h], vs.at[h], vr.at[h],
+                device_id={"layer": partner(my_layer, 1, n_layer)}, device_id_type=MESH))
+
+    def send(h, d):
+        if not chained or d == 1:
+            direct[h][d].start()
+        elif d == 3:
+            pl.when(at_end)(handed[h].start)
+            pl.when(inside)(direct[h][3].start)
+        else:
+            pl.when(at_end)(direct[h][2].start)
+
+    def hand_on(h):
+        if chained:
+            @pl.when(inside)
+            def _():
+                handed[h].wait_recv()
+                c_send[h, 1] = (c_send[h, 1].astype(jnp.float32) + via[h].astype(jnp.float32)).astype(jnp.bfloat16)
+                direct[h][2].start()
+
     for h in range(2):
         for d in range(1, n_row):
             receive(h, d)
+            if h == 1 and d == n_row - 2:
+                hand_on(0)
         for d in range(n_layer - 1, 0, -1):
             dst = partner(my_layer, d, n_layer)
             for o in range(own_rows):
@@ -210,24 +244,23 @@
                 for u in range(kc // 4):
                     c_send[h, d - 1, o, :, u * LANES:(u + 1) * LANES] = pick(
                         h, dst * own_rows + o, u).astype(jnp.bfloat16)
-            copy = pltpu.make_async_remote_copy(
-                c_send.at[h, d - 1], c_recv.at[h, d - 1], zs.at[h, d - 1], zr.at[h, d - 1],
-                device_id={"layer": dst}, device_id_type=MESH)
-            copy.start()
-            z_copies[h].append(copy)
-            sends.append(copy)
+            send(h, d)
         for o in range(own_rows):
             turn_row(h, my_layer * own_rows + o)
             for u in range(kc // 4):
                 own[h, o, :, u * LANES:(u + 1) * LANES] = pick(h, my_layer * own_rows + o, u)
-
-    for h in range(2):
-        for copy in z_copies[h]:
-            copy.wait_recv()
-        total = own[h]
+    hand_on(1)
+
+    def add(h, d):
+        direct[h][d].wait_recv()
+        own[h] = own[h] + c_recv[h, d - 1].astype(jnp.float32)
+
+    for h in range(2):
         for d in range(1, n_layer):
-            total = total + c_recv[h, d - 1].astype(jnp.float32)
-        own[h] = total
+            if chained and d == 3:
+                pl.when(inside)(functools.partial(add, h, 3))
+            else:
+                add(h, d)
     for o in range(own_rows):
         for u in range(kc // 4):
             h0 = own[0, o, :, u * LANES:(u + 1) * LANES]
@@ -237,6 +270,13 @@
                 out_ref[0, o, :, at:at + LANES] = tile.astype(jnp.bfloat16)
     for copy in sends:
         copy.wait_send()
+    for h in range(2):
+        for d in range(1, n_layer):
+            if chained and d == 3:
+                pl.when(at_end)(handed[h].wait_send)
+                pl.when(inside)(direct[h][3].wait_send)
+            else:
+                direct[h][d].wait_send()
 
 
 def local(dims, a_blocks, a_cols, p_blocks, p_cols, c_cols):
@@ -269,11 +309,13 @@
             pltpu.VMEM((2,) + half_strip, jnp.float32),
             pltpu.VMEM((2, n_layer - 1) + half_strip, jnp.bfloat16),
             pltpu.VMEM((2, n_layer - 1) + half_strip, jnp.bfloat16),
+            pltpu.VMEM((2,) + half_strip, jnp.bfloat16),
             dma((5,)),
             dma((2, n_row - 1)), dma((2, n_row - 1)),
             dma((n_row - 1,)), dma((n_row - 1,)),
             dma((n_col - 1,)), dma((n_col - 1,)),
             dma((2, n_layer - 1)), dma((2, n_layer - 1)),
+            dma((2,)), dma((2,)),
         ],
         compiler_params=pltpu.CompilerParams(
             collective_id=0, has_side_effects=True, vmem_limit_bytes=63 * 2**20),

time: 21.5 us -> 23 us (1.070)
  Pallas kernels: 19.8 us -> 21.4 us
    pallas_call x1, Pallas kernels: 19.8 us -> 21.4 us  [local(): pl.pallas_call(functools.partial(kernel, dims), out_shape=jax.ShapeDtypeS...]
where the time goes in v1:
time: 23 us; the launch traced here: 22.8 us
  Pallas kernels  21.4 us (93%)
  local copies, waits for them, and re-layouts  1.47 us (6%)
    pallas_call x1, Pallas kernels, local(): pl.pallas_call(functools.partial(kernel, dims), out_shape=jax.ShapeDtypeS...  21.4 us
    unnamed x1, local copies, waits for them, and re-layouts  1.47 us

profile of v1, /device:TPU:0, one launch (start us, length us, event | category | flops | bytes accessed | tf_op | source)
XLA Modules:
  0.0 22.8 jit_solution(1483605592699625076)
XLA Ops:
  0.0 21.4 %shard_map.55 = bf16[1,1,64,512]{3,2,1,0:T(8,128)(2,1)} custom-call(bf16[1,2,2,64,512]{4,3,2,1,0:T(8,128)(2,1)} %a_hbm.1, s32[1,2,2,8]{3,2,1,0:T(2,128)} %a_cols_hbm.1, bf16[1,2,1,2,64,256]{5,4,3,2,1,0:T(8,128)(2,1)} %p_hbm.1, s32[1,2,1,2,4]{4,3,2,1,0:T(2,128)} %p_cols_hbm.1, s32[1,4,8]{2,1,0:T(4,128)} %c_cols_hbm.1), custom_call_target="tpu_custom_call" | custom-call | tf_op jit(solution)/shard_map/pallas_call | solution.py:292
  21.4 1.5 %copy.7 = bf16[1,1,64,512]{3,2,1,0:T(8,128)(2,1)} copy(bf16[1,1,64,512]{3,2,1,0:T(8,128)(2,1)} %shard_map.55) | data formatting | bytes 131072

commit v2 on v0

--- a/solution.py
+++ b/solution.py
@@ -192,15 +192,16 @@
         spread_rows(h, partner(my_row, d, n_row), d)
         multiply(h, d)
 
-    for h in range(2):
-        spread_rows(h, my_row, 0)
+    spread_rows(0, my_row, 0)
     for copy in a_copies:
         copy.wait_recv()
-    for h in range(2):
-        multiply(h, 0)
+    multiply(0, 0)
 
     z_copies = [[], []]
     for h in range(2):
+        if h == 1:
+            spread_rows(1, my_row, 0)
+            multiply(1, 0)
         for d in range(1, n_row):
             receive(h, d)
         for d in range(n_layer - 1, 0, -1):

time: 21.5 us -> 21.5 us (level)
  no operation moved by 1% of the time
where the time goes in v2:
time: 21.5 us; the launch traced here: 21.3 us
  Pallas kernels  19.8 us (92%)
  local copies, waits for them, and re-layouts  1.47 us (7%)
    pallas_call x1, Pallas kernels, local(): pl.pallas_call(functools.partial(kernel, dims), out_shape=jax.ShapeDtypeS...  19.8 us
    unnamed x1, local copies, waits for them, and re-layouts  1.47 us

profile of v2, /device:TPU:0, one launch (start us, length us, event | category | flops | bytes accessed | tf_op | source)
XLA Modules:
  0.0 21.3 jit_solution(5211052848280190945)
XLA Ops:
  0.0 19.8 %shard_map.55 = bf16[1,1,64,512]{3,2,1,0:T(8,128)(2,1)} custom-call(bf16[1,2,2,64,512]{4,3,2,1,0:T(8,128)(2,1)} %a_hbm.1, s32[1,2,2,8]{3,2,1,0:T(2,128)} %a_cols_hbm.1, bf16[1,2,1,2,64,256]{5,4,3,2,1,0:T(8,128)(2,1)} %p_hbm.1, s32[1,2,1,2,4]{4,3,2,1,0:T(2,128)} %p_cols_hbm.1, s32[1,4,8]{2,1,0:T(4,128)} %c_cols_hbm.1), custom_call_target="tpu_custom_call" | custom-call | tf_op jit(solution)/shard_map/pallas_call | solution.py:253
  19.8 1.5 %copy.7 = bf16[1,1,64,512]{3,2,1,0:T(8,128)(2,1)} copy(bf16[1,1,64,512]{3,2,1,0:T(8,128)(2,1)} %shard_map.55) | data formatting | bytes 131072
